TPU v7x, 768 devices: a whole 4x8x12 slice. The times are simulated.
768 devices in a mesh: blk: 32 (over y, z_hi, core), rep: 24 (over z_lo, x).
Axes of the slice: x: 4, y: 8, z: 12 (z_hi: 2, z_lo: 6; z = z_hi * 6 + z_lo), core: 2. Of those that a mesh axis runs over, the one named last changes fastest.
Arguments:
- features: bfloat16 [98304, 256], P('blk'), may hold values from -6 to 6
- tiles: bfloat16 [32, 32, 24, 4, 128, 128], P('blk', None, 'rep'), may hold values from -0.06591797 to 0.06591797
- tile_rows: int32 [32, 32, 24, 4], P('blk', None, 'rep'), may hold values from 0 to 23
- tile_count: int32 [32, 32, 24], P('blk', None, 'rep'), may hold values from 1 to 4, as said below
- weight: bfloat16 [256, 256], replicated, may hold values from -0.375 to 0.375
- cotangent: bfloat16 [98304, 256], P('blk'), may hold values from -6 to 6
Outputs:
- activation: bfloat16 [98304, 256], P(('blk', 'rep'))
- grad_features: bfloat16 [98304, 256], P(('blk', 'rep'))
- grad_weight: float32 [256, 256], replicated
Inputs may be any that keep to these rules, and one draw needn't show every extreme that they name: `tile_count`: each live count is 1 to 4; the pair of a row block with itself has 4 in every column part.
All inputs are finite; a program needn't handle non-finite values.
Results may differ from a plain program's by a relative error of at most 0.035.
Values may be sent and summed in bfloat16 or wider, within the bound.
A program may use at most 64 MiB of HBM per device.

v0:
```python
import jax
import jax.numpy as jnp
from jax import lax
from jax.sharding import PartitionSpec as P


def dense_step(summed, weight, cot_rows):
    agg = summed.astype(jnp.bfloat16)
    pre = jnp.dot(agg, weight, preferred_element_type=jnp.float32)
    sig = jax.nn.sigmoid(pre)
    activ = (pre * sig).astype(jnp.bfloat16)
    dpre = (cot_rows.astype(jnp.float32) * sig * (1.0 + pre * (1.0 - sig))).astype(jnp.bfloat16)
    back = lax.dot_general(
        dpre, weight, (((1,), (1,)), ((), ())), preferred_element_type=jnp.float32
    )
    return (agg, activ, dpre, back.astype(jnp.bfloat16))


def body(features, tiles, tile_rows, tile_count, weight, cotangent):
    parts = lax.axis_size("rep")
    rep_index = lax.axis_index("rep")
    block = features.shape[0]
    width = features.shape[1]
    side = block // parts
    local = tiles[0, :, 0]
    rows_here = tile_rows[0, :, 0]
    count_here = tile_count[0, :, 0]
    slots = jnp.arange(local.shape[1], dtype=jnp.int32)
    live = slots[None, :] < count_here[:, None]
    hits = rows_here[:, :, None] == jnp.arange(parts, dtype=jnp.int32)[None, None, :]
    place = hits & live[:, :, None]
    place_f = place.astype(jnp.float32)
    place_b = place.astype(jnp.bfloat16)
    own = lax.dynamic_slice_in_dim(features, rep_index * side, side, 0)
    piece = lax.all_gather(own, "blk", axis=0, tiled=True)
    number = piece.shape[0] // side
    part_tiles = local
    shaped = piece.reshape(number, side, width)
    prod = jnp.einsum("ckij,cjf->ckif", part_tiles, shaped, preferred_element_type=jnp.float32)
    partial_value = jnp.einsum("ckt,ckif->tif", place_f, prod).reshape(block, width)
    summed = lax.psum_scatter(
        partial_value.astype(jnp.bfloat16), "rep", scatter_dimension=0, tiled=True
    ).astype(jnp.float32)
    cot_rows = lax.dynamic_slice_in_dim(cotangent, rep_index * side, side, 0)
    agg_rows, activation, dpre_rows, back_rows = dense_step(summed, weight, cot_rows)
    gathered = lax.all_gather(back_rows, "rep", axis=0, tiled=True)
    weight_part = lax.dot_general(
        agg_rows, dpre_rows, (((0,), (0,)), ((), ())), preferred_element_type=jnp.float32
    )
    grad_weight = lax.psum(weight_part, ("blk", "rep"))
    shaped_back = gathered.reshape(parts, side, width)
    picked = jnp.einsum(
        "ckt,tif->ckif", place_b, shaped_back, preferred_element_type=jnp.float32
    ).astype(jnp.bfloat16)
    part_tiles = local
    terms = jnp.einsum("ckij,ckif->cjf", part_tiles, picked, preferred_element_type=jnp.float32)
    grad_rows = lax.psum_scatter(
        terms.reshape(lax.axis_size("blk") * side, width).astype(jnp.bfloat16),
        "blk",
        scatter_dimension=0,
        tiled=True,
    )
    return (activation, grad_rows, grad_weight)


def solution(mesh):
    placed = (
        P("blk", None),
        P("blk", None, "rep", None, None, None),
        P("blk", None, "rep", None),
        P("blk", None, "rep"),
        P(),
        P("blk", None),
    )
    return jax.shard_map(
        body,
        mesh=mesh,
        in_specs=placed,
        out_specs=(P(("blk", "rep"), None), P(("blk", "rep"), None), P()),
        check_vma=False,
    )
```

profile of v0, /device:TPU:4, one launch (start us, length us, event | category | flops | bytes accessed | tf_op | source)
XLA Modules:
  0.0 1097.2 jit_solution(11652312046644542911)
XLA Ops:
  7.2 0.0 copy-start
  7.2 0.0 all-gather.3.cloned.1.call-start
  7.2 1.3 copy-done
  8.6 0.6 constant_dynamic-slice_fusion
  9.2 0.0 all-gather.3.cloned.1.call-update
  9.2 0.0 reduce-scatter.3.cloned.1.call-start
  9.3 0.7 iota_compare_fusion.1
  9.9 117.6 %all-gather.3.cloned.1.call-done = bf16[4096,256]{1,0:T(8,128)(2,1)} async-done(((bf16[128,256]{1,0:T(8,128)(2,1)}), bf16[4096,256]{1,0:T(8,128)(2,1)}) %all-gather.3.cloned.1.call-update) | async-done | bytes 2097168 | tf_op jit(solution)/shard_map/all_gather | solution.py:35
  127.5 8.4 fusion.4
  136.0 0.0 copy-start.2
  136.0 14.6 %copy.13 = bf16[32,256,4,128]{1,0,2,3:T(8,128)(2,1)} copy(bf16[32,256,4,128]{3,1,2,0:T(8,128)(2,1)} %fusion.4) | data formatting | bytes 16777216 | tf_op jit(solution)/shard_map/ckij,cjf->ckif/dot_general | solution.py:39
  150.6 0.0 copy-done.2
  150.6 4.9 bitcast_convert_fusion.1
  155.5 0.0 copy-start.1
  155.5 1.5 copy.10
  157.0 0.0 reduce-scatter.3.cloned.1.call-update
  157.0 0.0 all-gather.5.cloned.1.call-start
  157.1 148.6 %reduce-scatter.3.cloned.1.call-done = bf16[128,256]{1,0:T(8,128)(2,1)} async-done(((bf16[3072,256]{1,0:T(8,128)(2,1)}), bf16[128,256]{1,0:T(8,128)(2,1)}) %reduce-scatter.3.cloned.1.call-update) | async-done | bytes 65552 | tf_op jit(solution)/shard_map/reduce_scatter | solution.py:41
  305.7 0.0 copy-done.1
  305.7 1.7 multiply_convert_fusion
  307.4 0.8 convolution_convert_fusion
  308.3 0.0 all-gather.5.cloned.1.call-update
  308.3 0.0 all-reduce.2.cloned.1.call-start
  308.3 1.8 fusion.21
  310.1 0.0 all-reduce.2.cloned.1.call-update
  310.1 0.2 reduce-scatter.5.cloned.1.call-start
  310.4 150.4 %all-gather.5.cloned.1.call-done = bf16[3072,256]{1,0:T(8,128)(2,1)} async-done(((bf16[128,256]{1,0:T(8,128)(2,1)}), bf16[3072,256]{1,0:T(8,128)(2,1)}) %all-gather.5.cloned.1.call-update) | async-done | bytes 1572880 | tf_op jit(solution)/shard_map/all_gather | solution.py:46
  460.7 6.0 fusion.10
  466.8 15.4 %bitcast_convert_fusion = bf16[32,256,128]{1,2,0:T(8,128)(2,1)} fusion(bf16[1,32,1,4,128,128]{5,4,3,2,1,0:T(8,128)(2,1)} %param.7, bf16[32,4,128,256]{3,0,2,1:T(8,128)(2,1)} %fusion.10), kind=kOutput, calls=%fused_computation.4 | convolution fusion | flops 1074790400 | bytes 14680064 | tf_op jit(solution)/shard_map/ckij,ckif->cjf/dot_general | solution.py:56
  482.2 0.0 reduce-scatter.5.cloned.1.call-update
  482.3 449.3 %all-reduce.2.cloned.1.call-done = f32[256,256]{1,0:T(8,128)} async-done(((f32[256,256]{1,0:T(8,128)}), f32[256,256]{1,0:T(8,128)}) %all-reduce.2.cloned.1.call-update) | async-done | bytes 262160 | tf_op jit(solution)/shard_map/psum | solution.py:50
  931.6 157.4 %reduce-scatter.5.cloned.1.call-done = bf16[128,256]{1,0:T(8,128)(2,1)} async-done(((bf16[4096,256]{1,0:T(8,128)(2,1)}), bf16[128,256]{1,0:T(8,128)(2,1)}) %reduce-scatter.5.cloned.1.call-update) | async-done | bytes 65552 | tf_op jit(solution)/shard_map/reduce_scatter | solution.py:57
  1089.0 1.7 copy.27
Async XLA Ops:
  7.2 1.4 copy-start
  7.2 120.4 %all-gather.3.cloned.1.call-start = ((), (), s32[]{:S(2)}) async-start(), calls=%async_computation.2 | async-start | bytes 2162688 | tf_op jit(solution)/shard_map/all_gather | solution.py:35
  9.2 296.5 %reduce-scatter.3.cloned.1.call-start = ((), (), s32[]{:S(2)}) async-start(), calls=%async_computation.3 | async-start | bytes 1638400 | tf_op jit(solution)/shard_map/reduce_scatter | solution.py:41
  136.0 14.6 %copy-start.2 = (s32[1,32,1,4]{1,3,2,0:T(4,128)S(1)}, s32[1,32,1,4]{1,3,2,0:T(4,128)}, u32[]{:S(2)}) copy-start(s32[1,32,1,4]{1,3,2,0:T(4,128)} %param.8) | copy-start | bytes 1540
  155.5 150.2 %copy-start.1 = (bf16[256,256]{1,0:T(8,128)(2,1)S(1)}, bf16[256,256]{1,0:T(8,128)(2,1)}, u32[]{:S(2)}) copy-start(bf16[256,256]{1,0:T(8,128)(2,1)} %param.10) | copy-start | bytes 393220
  157.0 303.7 %all-gather.5.cloned.1.call-start = ((), (), s32[]{:S(2)}) async-start(), calls=%async_computation.4 | async-start | bytes 1638400 | tf_op jit(solution)/shard_map/all_gather | solution.py:46
  308.3 623.3 %all-reduce.2.cloned.1.call-start = ((), (), s32[]{:S(2)}) async-start(), calls=%async_computation.6 | async-start | bytes 524288 | tf_op jit(solution)/shard_map/psum | solution.py:50
  310.1 778.8 %reduce-scatter.5.cloned.1.call-start = ((), (), s32[]{:S(2)}) async-start(), calls=%async_computation.5 | async-start | bytes 2162688 | tf_op jit(solution)/shard_map/reduce_scatter | solution.py:57
Sparse Core Ops, SparseCore 0:
  12.5 114.9 all-gather.2
  157.2 148.5 reduce-scatter.2
  309.0 151.7 all-gather.4
  467.5 464.0 all-reduce.1
  937.2 151.6 reduce-scatter.4
where the time goes:
time: 1100 us
  waiting for transfers between devices  1020 us (93%)
  matrix products  39.1 us (4%)
  local copies, waits for them, and re-layouts  19.8 us (2%)
  between operations  13.8 us (1%)
    psum x1, waiting for transfers between devices, body(): grad_weight = lax.psum(weight_part, ('blk', 'rep'))  449 us
    reduce_scatter x1, waiting for transfers between devices, body(): lax.psum_scatter(terms.reshape(lax.axis_size('blk') * side, width).astype...  157 us
    all_gather x1, waiting for transfers between devices, body(): gathered = lax.all_gather(back_rows, 'rep', axis=0, tiled=True)  150 us
    reduce_scatter x1, waiting for transfers between devices, body(): lax.psum_scatter(partial_value.astype(jnp.bfloat16), 'rep', scatter_dimen...  149 us
    all_gather x1, waiting for transfers between devices, body(): piece = lax.all_gather(own, 'blk', axis=0, tiled=True)  118 us
  transfers between devices with their start and end apart: 5, of which 5 were waited for; matrix products, arithmetic and copies ran while one was open for 2% of the time, Pallas kernels for 0%

commit v1 on v0

v1 whole, which is shorter than its diff:
```python
import functools

import jax
import jax.numpy as jnp
from jax import lax
from jax.experimental import pallas as pl
from jax.experimental.pallas import tpu as pltpu
from jax.sharding import PartitionSpec as P

NX, NY, NZ = 4, 8, 6
SIDE, WIDTH, PARTS, BLOCKS, SLOTS = 128, 256, 24, 32, 4
MESH = pl.DeviceIdType.MESH
BF, F32 = jnp.bfloat16, jnp.float32
VMEM = pl.BlockSpec(memory_space=pltpu.VMEM)
SMEM = pl.BlockSpec(memory_space=pltpu.SMEM)
ANY = pl.BlockSpec(memory_space=pl.ANY)


class Place:
    def __init__(self):
        self.b = lax.axis_index("blk")
        self.r = lax.axis_index("rep")
        self.y = lax.div(self.b, 4)
        self.h = lax.rem(lax.div(self.b, 2), 2)
        self.c = lax.rem(self.b, 2)
        self.z = lax.div(self.r, NX)
        self.x = lax.rem(self.r, NX)

    def blk(self, dy=0, e=0, flip=0):
        y = lax.rem(self.y + dy + NY, NY)
        h = 1 - self.h if e else self.h
        c = 1 - self.c if flip else self.c
        return (y * 2 + h) * 2 + c

    def rep(self, dz=0, dx=0):
        return lax.rem(self.z + dz + NZ, NZ) * NX + lax.rem(self.x + dx + NX, NX)


def greet(peers):
    barrier = pltpu.get_barrier_semaphore()
    for peer in peers:
        pl.semaphore_signal(barrier, inc=1, device_id=peer, device_id_type=MESH)
    pl.semaphore_wait(barrier, len(peers))


def remote(src, dst, send_sem, recv_sem, device):
    return pltpu.make_async_remote_copy(
        src_ref=src, dst_ref=dst, send_sem=send_sem, recv_sem=recv_sem,
        device_id=device, device_id_type=MESH,
    )


def gather_kernel(feat, out, send_sem, recv_sem, own_sem):
    me = Place()
    sibling = (me.blk(flip=1), me.r)
    up, down = (me.blk(dy=1), me.r), (me.blk(dy=-1), me.r)
    far = me.rep(dz=3)
    partner = (me.blk(e=1), far)
    greet([sibling, up, down, partner])
    sends = []

    def start(src, slot, lane, device):
        copy = remote(src, out.at[slot], send_sem.at[len(sends)], recv_sem.at[slot], device)
        copy.start()
        sends.append(copy)

    def arrive(slot):
        remote(out.at[slot], out.at[slot], send_sem.at[0], recv_sem.at[slot], sibling).wait_recv()

    own = feat.at[pl.ds(me.r * SIDE, SIDE), :]
    start(feat.at[pl.ds(far * SIDE, SIDE), :], me.b, 0, partner)
    start(own, me.b, 1, up)
    start(own, me.b, 2, down)
    start(own, me.b, 3, sibling)
    local = pltpu.make_async_copy(own, out.at[me.b], own_sem)
    local.start()
    crossed = me.blk(e=1)
    arrive(crossed)
    start(out.at[crossed], crossed, 0, up)
    start(out.at[crossed], crossed, 1, down)
    start(out.at[crossed], crossed, 2, sibling)
    for far_y in (1, 2, 3, 4):
        for e in (0, 1):
            for sign, onward, reach in ((-1, up, 3 + e), (1, down, 4 - e)):
                if far_y > reach:
                    continue
                slot = me.blk(dy=sign * far_y, e=e)
                arrive(slot)
                if far_y < reach:
                    start(out.at[slot], slot, 0, onward)
                start(out.at[slot], slot, 1, sibling)
    local.wait()
    for dy in range(NY):
        for e in (0, 1):
            arrive(me.blk(dy=dy, e=e, flip=1))
    for copy in sends:
        copy.wait_send()


GATHER_SENDS = 4 + 3 + 14 + 12


def forward_kernel(index, tiles, feats, out, total):
    total[...] = jnp.zeros_like(total)

    def column(c, carry):
        x = feats[c]
        for k in range(SLOTS):
            t = index[c * SLOTS + k]

            @pl.when(t < PARTS)
            def _():
                total[t] += jnp.dot(tiles[c, k], x, preferred_element_type=F32)

        return carry

    lax.fori_loop(0, BLOCKS, column, 0)
    out[...] = total[...].astype(BF)


Z_ORDER = (3, 2, 4, 1, 5, 0)


def group_of(p):
    m, e = 4 - lax.div(p, 4), 1 - lax.rem(p, 2)
    dy = jnp.where(lax.rem(p, 4) < 2, m, -m)
    return dy, e


GROUPS = [(m if p % 4 < 2 else -m, 1 - p % 2) for p in range(2, 18) for m in [4 - p // 4]]
HOPS = [(sign, e, m) for m in (4, 3, 2, 1) for e in (1, 0) for sign in (1, -1)
        if m <= (3 + e if sign > 0 else 4 - e)]


def back_kernel(
    index, part, tiles_hbm, weight, cot_hbm,
    act_out, grad_out, weight_out,
    tiles, cot, got_x, sum_z, got_z, back, to_core, from_core, mine, ring_out, ring_in,
    cross_out, cross_in, wsum, w1_out, w1_in, w2_out, w2_in, w3_out, w3_in, w4_out, w4_in, w5_in, w6_in,
    local_sem, rx_s, rx_r, rz_s, rz_r, gz_s, gz_r, gx_s, gx_r, core_s, core_r, ring_s, ring_r,
    cross_s, cross_r, wa_s, wa_r, wy_s, wy_r, wx_s, wx_r, wz_s, wz_r, wo_s, wo_r,
):
    me = Place()
    sibling = (me.blk(flip=1), me.r)
    up, down = (me.blk(dy=1), me.r), (me.blk(dy=-1), me.r)
    other = (me.blk(e=1), me.r)
    peers = [sibling]
    peers += [(me.blk(dy=dy), me.r) for dy in range(1, NY)]
    peers += [(me.b, me.rep(dx=dx)) for dx in range(1, NX)]
    peers += [(me.blk(e=e), me.rep(dz=dz)) for e in (0, 1) for dz in range(NZ) if e or dz]

    load_tiles = pltpu.make_async_copy(tiles_hbm.at[0, :, 0], tiles, local_sem.at[0])
    load_tiles.start()
    load_cot = pltpu.make_async_copy(cot_hbm.at[pl.ds(me.r * SIDE, SIDE), :], cot, local_sem.at[1])
    load_cot.start()
    greet(peers)
    sends = []

    def start(*args):
        copy = remote(*args)
        copy.start()
        sends.append(copy)

    def arrive(dst, sem):
        remote(dst, dst, local_sem.at[2], sem, sibling).wait_recv()

    for o in Z_ORDER:
        for dx in (1, 3, 2):
            start(part.at[me.rep(dz=o, dx=dx)], got_x.at[o, dx], rx_s.at[o, dx], rx_r.at[o, dx],
                  (me.b, me.rep(dx=dx)))
    for o in Z_ORDER:
        value = part[me.rep(dz=o)].astype(F32)
        for dx in (1, 3, 2):
            arrive(got_x.at[o, dx], rx_r.at[o, dx])
            value += got_x[o, dx].astype(F32)
        if o:
            sum_z[o] = value.astype(BF)
            start(sum_z.at[o], got_z.at[o], rz_s.at[o], rz_r.at[o], (me.b, me.rep(dz=o)))
    for o in range(1, NZ):
        arrive(got_z.at[o], rz_r.at[o])
        value += got_z[o].astype(F32)

    load_cot.wait()
    agg = value.astype(BF)
    pre = jnp.dot(agg, weight[...], preferred_element_type=F32)
    sig = jax.nn.sigmoid(pre)
    dpre = (cot[...].astype(F32) * sig * (1.0 + pre * (1.0 - sig))).astype(BF)
    back[me.r] = lax.dot_general(
        dpre, weight[...], (((1,), (1,)), ((), ())), preferred_element_type=F32
    ).astype(BF)

    def over_x(o):
        slot = back.at[me.rep(dz=o)]
        start(slot, slot, gx_s.at[o, 1], gx_r.at[o, 1], (me.b, me.rep(dx=1)))
        start(slot, slot, gx_s.at[o, 3], gx_r.at[o, 3], (me.b, me.rep(dx=-1)))

    mine_back = back.at[me.r]
    for o in (1, 5, 2, 4, 3):
        start(mine_back, mine_back, gz_s.at[o], gz_r.at[o], (me.b, me.rep(dz=-o)))
        if o == 1:
            over_x(0)

    act_out[...] = (pre * sig).astype(BF)
    wsum[...] = lax.dot_general(agg, dpre, (((0,), (0,)), ((), ())), preferred_element_type=F32)
    half = SIDE
    w1_out[...] = wsum[pl.ds((1 - me.c) * half, half), :].astype(BF)
    start(w1_out, w1_in, wa_s.at[0], wa_r.at[0], sibling)
    back[PARTS] = jnp.zeros((SIDE, WIDTH), BF)

    def relay(o):
        near, onward = (1, 1) if o % 2 == 0 else (3, -1)
        slot = back.at[me.rep(dz=o, dx=-near)]
        arrive(slot, gx_r.at[o, near])
        start(slot, slot, gx_s.at[o, 2], gx_r.at[o, 2], (me.b, me.rep(dx=onward)))

    for o in (1, 5, 2, 4, 3):
        arrive(back.at[me.rep(dz=o)], gz_r.at[o])
        over_x(o)
        if o == 1:
            relay(0)
            arrive(w1_in, wa_r.at[0])
            w1 = wsum[pl.ds(me.c * half, half), :] + w1_in[...].astype(F32)
            wsum[0:half, :] = w1
            w2_out[...] = w1.astype(BF).reshape(NY, 16, WIDTH)
            for dy in range(1, NY):
                start(w2_out.at[lax.rem(me.y + dy, NY)], w2_in.at[dy], wy_s.at[dy], wy_r.at[dy],
                      (me.blk(dy=dy), me.r))
    for o in (1, 5, 2, 4, 3):
        relay(o)

    w2 = wsum[pl.ds(me.y * 16, 16), :]
    for dy in range(1, NY):
        arrive(w2_in.at[dy], wy_r.at[dy])
        w2 += w2_in[dy].astype(F32)
    w3_in[me.x] = w2.astype(BF)
    for dx in range(1, NX):
        slot = w3_in.at[me.x]
        start(slot, slot, wx_s.at[dx], wx_r.at[dx], (me.b, me.rep(dx=dx)))

    for o in range(NZ):
        far = (3 if o % 2 == 0 else 1)
        arrive(back.at[me.rep(dz=o, dx=-far)], gx_r.at[o, far])
        arrive(back.at[me.rep(dz=o, dx=2)], gx_r.at[o, 2])
    load_tiles.wait()

    def term(c):
        picked = jnp.concatenate([back[index[c * SLOTS + k]] for k in range(SLOTS)], axis=0)
        return lax.dot_general(
            tiles[c].reshape(SLOTS * SIDE, SIDE), picked, (((0,), (0,)), ((), ())),
            preferred_element_type=F32,
        )

    def to_sibling(p):
        return remote(to_core.at[p], from_core.at[p], core_s.at[p], core_r.at[p], sibling)

    def terms(p, carry):
        dy, e = group_of(p)
        y = lax.rem(me.y + dy + NY, NY)
        h = jnp.where(e == 1, 1 - me.h, me.h)
        base = (y * 2 + h) * 2
        to_core[p - 2] = term(base + 1 - me.c).astype(BF)
        to_sibling(p - 2).start()
        mine[p - 2] = term(base + me.c)
        return carry

    def ring(p):
        dy, e = GROUPS[p]
        to_sibling(p).wait_recv()
        value = mine[p] + from_core[p].astype(F32)
        for sign, step in ((1, up), (-1, down)):
            m = sign * dy
            if abs(dy) == 4:
                m = 4 if (sign > 0) == (e == 1) else 9
            elif dy and m < 0:
                continue
            k = HOPS.index((sign, e, m + 1)) if (sign, e, m + 1) in HOPS else None
            if k is not None:
                arrive(ring_in.at[k], ring_r.at[k])
                value += ring_in[k].astype(F32)
            if (sign, e, m) in HOPS:
                k = HOPS.index((sign, e, m))
                ring_out[k] = value.astype(BF)
                start(ring_out.at[k], ring_in.at[k], ring_s.at[k], ring_r.at[k], step)
        return value

    lax.fori_loop(2, 4, terms, 0)
    ring(0)
    ring(1)
    lax.fori_loop(4, 18, terms, 0)

    w3 = None
    for dx in range(1, NX):
        slot = w3_in.at[lax.rem(me.x + NX - dx, NX)]
        arrive(slot, wx_r.at[dx])
    w3 = sum((w3_in[i].astype(F32) for i in range(1, NX)), w3_in[0].astype(F32))
    zed = me.h * NZ + me.z
    w4_in[zed] = w3.astype(BF)
    for e in (0, 1):
        for dz in range(NZ):
            if e or dz:
                slot = w4_in.at[zed]
                start(slot, slot, wz_s.at[e, dz], wz_r.at[e, dz], (me.blk(e=e), me.rep(dz=dz)))

    for p in range(2, 10):
        ring(p)

    for e in (0, 1):
        for dz in range(NZ):
            if e or dz:
                h = 1 - me.h if e else me.h
                slot = w4_in.at[h * NZ + lax.rem(me.z + NZ - dz, NZ)]
                arrive(slot, wz_r.at[e, dz])
    w4 = sum((w4_in[i].astype(F32) for i in range(1, 2 * NZ)), w4_in[0].astype(F32))
    w5_in[me.y] = w4.astype(BF)

    for p in range(10, 14):
        ring(p)
    cross_out[...] = ring(14).astype(BF)
    start(cross_out, cross_in, cross_s.at[0], cross_r.at[0], other)
    for dy in range(1, NY):
        slot = w5_in.at[me.y]
        start(slot, slot, wo_s.at[dy], wo_r.at[dy], (me.blk(dy=dy), me.r))
    value = ring(15)
    for dy in range(1, NY):
        arrive(w5_in.at[lax.rem(me.y + NY - dy, NY)], wo_r.at[dy])
    start(w5_in, w6_in, wa_s.at[1], wa_r.at[1], sibling)
    weight_out[pl.ds(me.c * half, half), :] = w5_in[...].astype(F32).reshape(half, WIDTH)
    arrive(w6_in, wa_r.at[1])
    weight_out[pl.ds((1 - me.c) * half, half), :] = w6_in[...].astype(F32).reshape(half, WIDTH)
    arrive(cross_in, cross_r.at[0])
    grad_out[...] = (value + cross_in[...].astype(F32)).astype(BF)
    for copy in sends:
        copy.wait_send()

    def drain(p, carry):
        to_sibling(p).wait_send()
        return carry

    lax.fori_loop(0, 16, drain, 0)


def dma(*shape):
    return pltpu.SemaphoreType.DMA(shape)


def piece(*lead, dtype=BF):
    return pltpu.VMEM((*lead, SIDE, WIDTH), dtype)


def body(features, tiles, tile_rows, tile_count, weight, cotangent):
    slots = jnp.arange(SLOTS, dtype=jnp.int32)
    live = slots[None, :] < tile_count[0, :, 0][:, None]
    index = jnp.where(live, tile_rows[0, :, 0], PARTS).reshape(BLOCKS * SLOTS)

    gathered = pl.pallas_call(
        gather_kernel,
        out_shape=jax.ShapeDtypeStruct((BLOCKS, SIDE, WIDTH), BF),
        in_specs=[ANY],
        out_specs=VMEM,
        scratch_shapes=[dma(GATHER_SENDS), dma(BLOCKS), pltpu.SemaphoreType.DMA],
        compiler_params=pltpu.CompilerParams(
            collective_id=0, has_side_effects=True, vmem_limit_bytes=8 << 20
        ),
        name="gather_features",
    )(features)

    part = pl.pallas_call(
        forward_kernel,
        out_shape=jax.ShapeDtypeStruct((PARTS, SIDE, WIDTH), BF),
        in_specs=[SMEM, VMEM, VMEM],
        out_specs=VMEM,
        scratch_shapes=[piece(PARTS, dtype=F32)],
        compiler_params=pltpu.CompilerParams(vmem_limit_bytes=24 << 20),
        name="forward_tiles",
    )(index, tiles.reshape(BLOCKS, SLOTS, SIDE, SIDE), gathered)

    small = pltpu.VMEM((NY, 16, WIDTH), BF)
    activation, grad_rows, grad_weight = pl.pallas_call(
        back_kernel,
        out_shape=(
            jax.ShapeDtypeStruct((SIDE, WIDTH), BF),
            jax.ShapeDtypeStruct((SIDE, WIDTH), BF),
            jax.ShapeDtypeStruct((WIDTH, WIDTH), F32),
        ),
        in_specs=[SMEM, VMEM, ANY, VMEM, ANY],
        out_specs=(VMEM, VMEM, VMEM),
        scratch_shapes=[
            pltpu.VMEM((BLOCKS, SLOTS, SIDE, SIDE), BF),
            piece(),
            piece(NZ, NX), piece(NZ), piece(NZ),
            piece(PARTS + 1),
            piece(16), piece(16), piece(16, dtype=F32),
            piece(len(HOPS)), piece(len(HOPS)),
            piece(), piece(),
            pltpu.VMEM((WIDTH, WIDTH), F32),
            piece(), piece(),
            small, small,
            pltpu.VMEM((16, WIDTH), BF), pltpu.VMEM((NX, 16, WIDTH), BF),
            pltpu.VMEM((16, WIDTH), BF), pltpu.VMEM((2 * NZ, 16, WIDTH), BF),
            small, small,
            dma(3),
            dma(NZ, NX), dma(NZ, NX), dma(NZ), dma(NZ),
            dma(NZ), dma(NZ), dma(NZ, NX), dma(NZ, NX),
            dma(16), dma(16), dma(len(HOPS)), dma(len(HOPS)),
            dma(1), dma(1), dma(2), dma(2),
            dma(NY), dma(NY), dma(NX), dma(NX), dma(2, NZ), dma(2, NZ), dma(NY), dma(NY),
        ],
        compiler_params=pltpu.CompilerParams(
            collective_id=1, has_side_effects=True, vmem_limit_bytes=40 << 20
        ),
        name="aggregate_and_back",
    )(index, part, tiles, weight, cotangent)
    return activation, grad_rows, grad_weight


def solution(mesh):
    placed = (
        P("blk", None),
        P("blk", None, "rep", None, None, None),
        P("blk", None, "rep", None),
        P("blk", None, "rep"),
        P(),
        P("blk", None),
    )
    return jax.shard_map(
        body,
        mesh=mesh,
        in_specs=placed,
        out_specs=(P(("blk", "rep"), None), P(("blk", "rep"), None), P()),
        check_vma=False,
    )
```

time: 1100 us -> 143 us (0.13)
  waiting for transfers between devices: 1020 us -> 0 us
  Pallas kernels: 0 us -> 135 us
  matrix products: 39.1 us -> 0 us
  local copies, waits for them, and re-layouts: 19.8 us -> 6.54 us
  between operations: 13.8 us -> 0.71 us
    psum x1 -> x0, waiting for transfers between devices: 449 us -> none  [body(): grad_weight = lax.psum(weight_part, ('blk', 'rep'))]
    reduce_scatter x2 -> x0, waiting for transfers between devices: 306 us -> none  [the longest x1 157 us: body(): lax.psum_scatter(terms.reshape(lax.axis_size('blk') * side, width).astype...]
    all_gather x2 -> x0, waiting for transfers between devices: 268 us -> none  [the longest x1 150 us: body(): gathered = lax.all_gather(back_rows, 'rep', axis=0, tiled=True)]
    pallas_call x0 -> x3, Pallas kernels: none -> 135 us  [the longest x1 90.5 us: body(): pl.pallas_call(back_kernel, out_shape=(jax.ShapeDtypeStruct((SIDE, WIDTH)...]
    dot_general x7 -> x0, matrix products: 39.1 us -> none  [the longest x1 15.4 us: body(): jnp.einsum('ckij,ckif->cjf', part_tiles, picked, preferred_element_type=j...]
    dot_general x1 -> x0, local copies, waits for them, and re-layouts: 14.6 us -> none  [body(): jnp.einsum('ckij,cjf->ckif', part_tiles, shaped, preferred_element_type=j...]
  transfers between devices with their start and end apart: 5 -> 0, of which waited for: 5 -> 0; matrix products, arithmetic and copies ran while one was open for 2% -> 0% of each run, Pallas kernels for 0% -> 0%
where the time goes in v1:
time: 143 us
  Pallas kernels  135 us (94%)
  local copies, waits for them, and re-layouts  6.54 us (5%)
    pallas_call x1, Pallas kernels, body(): pl.pallas_call(back_kernel, out_shape=(jax.ShapeDtypeStruct((SIDE, WIDTH)...  90.5 us
    pallas_call x1, Pallas kernels, body(): pl.pallas_call(gather_kernel, out_shape=jax.ShapeDtypeStruct((BLOCKS, SID...  34.4 us
    pallas_call x1, Pallas kernels, body(): pl.pallas_call(forward_kernel, out_shape=jax.ShapeDtypeStruct((PARTS, SID...  9.59 us
    unnamed x14, local copies, waits for them, and re-layouts  6.33 us

profile of v1, /device:TPU:4, one launch (start us, length us, event | category | flops | bytes accessed | tf_op | source)
XLA Modules:
  0.0 142.5 jit_solution(15441900716042354075)
XLA Ops:
  0.6 0.7 iota_compare_fusion
  1.4 0.1 lt.23
  1.5 0.8 copy.10
  2.2 0.1 squeeze.3
  2.4 0.0 copy-start.2
  2.4 1.4 copy-done.2
  3.8 34.4 %gather_features.1.feats = bf16[32,128,256]{2,1,0:T(8,128)(2,1)S(1)} custom-call(bf16[3072,256]{1,0:T(8,128)(2,1)S(1)} %copy-done.2), custom_call_target="tpu_custom_call" | custom-call | tf_op jit(solution)/shard_map/gather_features/pallas_call | solution.py:355
  38.2 0.0 copy-start
  38.2 2.2 %copy-done = bf16[1,32,1,4,128,128]{5,4,3,2,1,0:T(8,128)(2,1)S(1)} copy-done((bf16[1,32,1,4,128,128]{5,4,3,2,1,0:T(8,128)(2,1)S(1)}, bf16[1,32,1,4,128,128]{5,4,3,2,1,0:T(8,128)(2,1)}, u32[]{:S(2)}) %copy-start) | copy-done | bytes 4194328
  40.4 0.0 copy-start.1
  40.4 0.0 copy-start.3
  40.4 0.0 copy-start.4
  40.4 9.6 %forward_tiles.1.part = bf16[24,128,256]{2,1,0:T(8,128)(2,1)S(1)} custom-call(s32[128]{0:T(128)S(1)} %broadcast_select_fusion.index, bf16[32,4,128,128]{3,2,1,0:T(8,128)(2,1)S(1)} %bitcast.6, bf16[32,128,256]{2,1,0:T(8,128)(2,1)S(1)} %gather_features.1.feats), custom_call_target="tpu_custom_call" | custom-call | tf_op jit(solution)/shard_map/forward_tiles/pallas_call | solution.py:367
  50.0 0.0 copy-done.1
  50.0 0.0 copy-done.3
  50.0 0.0 copy-done.4
  50.0 90.5 %aggregate_and_back.1 = (bf16[128,256]{1,0:T(8,128)(2,1)S(1)}, bf16[128,256]{1,0:T(8,128)(2,1)S(1)}, f32[256,256]{1,0:T(8,128)S(1)}) custom-call(s32[128]{0:T(128)S(1)} %broadcast_select_fusion.index, bf16[24,128,256]{2,1,0:T(8,128)(2,1)S(1)} %forward_tiles.1.part, bf16[1,32,1,4,128,128]{5,4,3,2,1,0:T(8,128)(2,1)S(1)} %copy-done.1, ...), custom_call_target="tpu_custom_call" | custom-call | tf_op jit(solution)/shard_map/aggregate_and_back/pallas_call | solution.py:378
  140.5 0.6 copy.14
  141.2 0.6 copy.15
  141.8 0.7 copy.16
  (1 shorter events, 0.0 us)
Async XLA Ops:
  2.4 1.4 copy-start.2
  38.2 2.2 %copy-start = (bf16[1,32,1,4,128,128]{5,4,3,2,1,0:T(8,128)(2,1)S(1)}, bf16[1,32,1,4,128,128]{5,4,3,2,1,0:T(8,128)(2,1)}, u32[]{:S(2)}) copy-start(bf16[1,32,1,4,128,128]{5,4,3,2,1,0:T(8,128)(2,1)} %tiles_hbm.1) | copy-start | bytes 12582916
  40.4 9.6 %copy-start.1 = (bf16[1,32,1,4,128,128]{5,4,3,2,1,0:T(8,128)(2,1)S(1)}, bf16[1,32,1,4,128,128]{5,4,3,2,1,0:T(8,128)(2,1)}, u32[]{:S(2)}) copy-start(bf16[1,32,1,4,128,128]{5,4,3,2,1,0:T(8,128)(2,1)} %tiles_hbm.1) | copy-start | bytes 12582916
  40.4 9.6 %copy-start.3 = (bf16[3072,256]{1,0:T(8,128)(2,1)S(1)}, bf16[3072,256]{1,0:T(8,128)(2,1)}, u32[]{:S(2)}) copy-start(bf16[3072,256]{1,0:T(8,128)(2,1)} %cot_hbm.1) | copy-start | bytes 4718596
  40.4 9.6 %copy-start.4 = (bf16[256,256]{1,0:T(8,128)(2,1)S(1)}, bf16[256,256]{1,0:T(8,128)(2,1)}, u32[]{:S(2)}) copy-start(bf16[256,256]{1,0:T(8,128)(2,1)} %weight.1) | copy-start | bytes 393220

commit v2 on v1

v2 whole, which is shorter than its diff:
```python
import jax
import jax.numpy as jnp
from jax import lax
from jax.experimental import pallas as pl
from jax.experimental.pallas import tpu as pltpu
from jax.sharding import PartitionSpec as P

NX, NY, NZ = 4, 8, 6
SIDE, WIDTH, PARTS, BLOCKS, SLOTS = 128, 256, 24, 32, 4
MESH = pl.DeviceIdType.MESH
BF, F32 = jnp.bfloat16, jnp.float32
VMEM = pl.BlockSpec(memory_space=pltpu.VMEM)
SMEM = pl.BlockSpec(memory_space=pltpu.SMEM)
ANY = pl.BlockSpec(memory_space=pl.ANY)


class Place:
    def __init__(self):
        self.b = lax.axis_index("blk")
        self.r = lax.axis_index("rep")
        self.y = lax.div(self.b, 4)
        self.h = lax.rem(lax.div(self.b, 2), 2)
        self.c = lax.rem(self.b, 2)
        self.z = lax.div(self.r, NX)
        self.x = lax.rem(self.r, NX)

    def blk(self, dy=0, e=0, flip=0):
        y = lax.rem(self.y + dy + NY, NY)
        h = 1 - self.h if e else self.h
        c = 1 - self.c if flip else self.c
        return (y * 2 + h) * 2 + c

    def rep(self, dz=0, dx=0):
        return lax.rem(self.z + dz + NZ, NZ) * NX + lax.rem(self.x + dx + NX, NX)


def greet(peers):
    barrier = pltpu.get_barrier_semaphore()
    for peer in peers:
        pl.semaphore_signal(barrier, inc=1, device_id=peer, device_id_type=MESH)
    pl.semaphore_wait(barrier, len(peers))


def remote(src, dst, send_sem, recv_sem, device):
    return pltpu.make_async_remote_copy(
        src_ref=src, dst_ref=dst, send_sem=send_sem, recv_sem=recv_sem,
        device_id=device, device_id_type=MESH,
    )


NEAR = [sorted((z for z in range(NZ) if z != home), key=lambda z: abs(z - home)) for home in range(NZ)]
HOPS = [(e, dy) for dy in (4, 3, -3, 2, -2, 1, -1) for e in (1, 0)]
GROUPS = [(1, 4), (0, 4)] + [(e, s * m) for m in (3, 2, 1) for s in (1, -1) for e in (1, 0)] + [(1, 0), (0, 0)]


def choose(at, values):
    out = values[0]
    for i, value in enumerate(values[1:], 1):
        out = jnp.where(at == i, value, out)
    return out


def layer_kernel(
    rows, counts, feat, tiles_hbm, weight, cot_hbm,
    act_out, grad_out, weight_out,
    feats, tiles, tiles_t, prods, sums, part, marks, marks_s, cot,
    got_x, mid_x, sum_z, got_z, back, to_core, from_core, mine, ring_out, ring_in,
    cross_out, cross_in, wsum, w1_out, w1_in, w2_out, w2_in, w3_in, w4_in, w5_in, w6_in,
    local_sem, feat_s, feat_r, rx_s, rx_r, rz_s, rz_r, gz_s, gz_r, gx_s, gx_r, core_s, core_r, ring_s, ring_r,
    cross_s, cross_r, wa_s, wa_r, wy_s, wy_r, wx_s, wx_r, wz_s, wz_r, wo_s, wo_r,
):
    me = Place()
    sibling = (me.blk(flip=1), me.r)
    other = (me.blk(e=1), me.r)
    far = me.rep(dz=3)
    peers = [sibling]
    peers += [(me.blk(dy=dy), me.r) for dy in range(1, NY)]
    peers += [(me.b, me.rep(dx=dx)) for dx in range(1, NX)]
    peers += [(me.blk(e=e), me.rep(dz=dz)) for e in (0, 1) for dz in range(NZ) if e or dz]

    load_tiles = pltpu.make_async_copy(tiles_hbm.at[0, :, 0], tiles, local_sem.at[0])
    load_tiles.start()
    load_cot = pltpu.make_async_copy(cot_hbm.at[pl.ds(me.r * SIDE, SIDE), :], cot, local_sem.at[1])
    load_cot.start()
    own = feat.at[pl.ds(me.r * SIDE, SIDE), :]
    load_own = pltpu.make_async_copy(own, feats.at[me.b], local_sem.at[2])
    load_own.start()
    greet(peers)
    sends = []

    def start(*args):
        copy = remote(*args)
        copy.start()
        sends.append(copy)

    def arrive(dst, sem):
        remote(dst, dst, local_sem.at[3], sem, sibling).wait_recv()

    def feat_send(src, slot, lane, device):
        start(src, feats.at[slot], feat_s.at[lane, slot], feat_r.at[slot], device)

    def feat_arrive(slot):
        arrive(feats.at[slot], feat_r.at[slot])

    def feat_spread(src, slot):
        for n, dy in enumerate((2, -2, 1, -1)):
            feat_send(src, slot, n, (me.blk(dy=dy), me.r))
        feat_send(src, slot, 4, sibling)

    feat_send(feat.at[pl.ds(far * SIDE, SIDE), :], me.b, 5, (me.blk(e=1), far))
    feat_spread(own, me.b)

    lane = lax.broadcasted_iota(jnp.int32, (8, SIDE), 1)
    nought = jnp.zeros((8, SIDE), jnp.int32)

    def target(c, k):
        return jnp.where(k < counts[c], rows[k, c], PARTS)

    def slot_key(s):
        return target(lax.div(s, SLOTS), lax.rem(s, SLOTS))

    def spread(s, carry):
        unique, below, upto = carry
        key = slot_key(s)
        unique = jnp.where(lane == s, key * SIDE + s, unique)
        below += jnp.where(lane > key, 1, 0)
        upto += jnp.where(lane >= key, 1, 0)
        return unique, below, upto

    def rank_of(s, rank):
        return rank + jnp.where(unique > slot_key(s) * SIDE + s, 1, 0)

    def place(s, carry):
        order, keys = carry
        hit = lane == marks_s[0, 0, s]
        return jnp.where(hit, s, order), jnp.where(hit, slot_key(s), keys)

    sums[SIDE] = jnp.zeros((SIDE, WIDTH), BF)
    back[PARTS] = jnp.zeros((SIDE, WIDTH), BF)

    def turn(lo, hi):
        def body(c, carry):
            tiles_t[c] = tiles[c].reshape(SLOTS * SIDE, SIDE).T
            return carry

        lax.fori_loop(lo, hi, body, 0)

    def column(c):
        value = jnp.dot(tiles[c].reshape(SLOTS * SIDE, SIDE), feats[c], preferred_element_type=F32)
        prods[pl.ds(c * SLOTS, SLOTS)] = value.reshape(SLOTS, SIDE, WIDTH)

    def columns(which, flip):
        def body(j, carry):
            e, dy = (choose(j, v) for v in zip(*which))
            y = lax.rem(me.y + dy + NY, NY)
            h = jnp.where(e == 1, 1 - me.h, me.h)
            c = (y * 2 + h) * 2 + (1 - me.c if flip else me.c)
            if flip:
                feat_arrive(c)
            column(c)
            return carry

        lax.fori_loop(0, len(which), body, 0)

    def onward(e):
        for dy in (-2, 2):
            slot = me.blk(dy=dy, e=e)
            feat_arrive(slot)
            if (dy < 0) == (e == 1):
                feat_send(feats.at[slot], slot, 1 if dy > 0 else 0, (me.blk(dy=-dy), me.r))
            step = -1 if dy > 0 else 1
            feat_send(feats.at[slot], slot, 2, (me.blk(dy=step), me.r))
            feat_send(feats.at[slot], slot, 4, sibling)

    def settle(e, *dys):
        for dy in dys:
            slot = me.blk(dy=dy, e=e)
            feat_arrive(slot)
            feat_send(feats.at[slot], slot, 4, sibling)

    unique, below, upto = lax.fori_loop(0, SIDE, spread, (nought, nought, nought), unroll=8)
    onward(0)
    crossed = me.blk(e=1)
    feat_arrive(crossed)
    feat_spread(feats.at[crossed], crossed)
    settle(0, 1, -1)
    marks[0] = lax.fori_loop(0, SIDE, rank_of, nought, unroll=8)
    marks[3] = jnp.where(upto > below, upto - 1, SIDE)
    pltpu.sync_copy(marks.at[0], marks_s.at[0])
    onward(1)
    settle(1, 1, -1)
    settle(0, 3, -3, 4)
    order, keys = lax.fori_loop(0, SIDE, place, (nought, nought), unroll=8)
    marks[1] = order
    marks[2] = keys
    pltpu.sync_copy(marks.at[pl.ds(1, 3)], marks_s.at[pl.ds(1, 3)])
    load_tiles.wait()
    load_own.wait()
    early = [(0, 0), (1, 0)] + [(0, dy) for dy in (1, -1, 2, -2)] + [(1, dy) for dy in (1, -1, 2, -2)]
    late = [(0, 3), (0, -3), (0, 4), (1, 3), (1, -3), (1, 4)]
    columns(early + late[:3], 0)
    settle(1, 3, -3, 4)
    columns(early, 1)
    columns(late[3:], 0)
    columns(late, 1)

    for lo in range(0, SIDE, 64):
        span = slice(lo, lo + 64)

        def scan(p, total):
            key = marks_s[2, 0, p]
            before = marks_s[2, 0, jnp.maximum(p - 1, 0)]
            keep = jnp.where(key == before, 1.0, 0.0).astype(F32)
            total = total * keep + prods[marks_s[1, 0, p], span, :]
            sums[p, span, :] = total.astype(BF)
            return total

        lax.fori_loop(0, SIDE, scan, jnp.zeros((64, WIDTH), F32), unroll=4)

    def pick(t):
        part[t] = sums[marks_s[3, 0, t]]

    at_z = [choose(me.z, [NEAR[home][NZ - 2 - k] for home in range(NZ)]) for k in range(NZ - 1)] + [me.z]

    def tile_at(k, dx=0):
        return at_z[k] * NX + lax.rem(me.x + dx + NX, NX)

    def ways(k):
        return 1 if k % 2 == 0 else -1

    def toward(dx):
        return (me.b, me.rep(dx=dx))

    for k in range(NZ):
        pick(tile_at(k, 2))
        start(part.at[tile_at(k, 2)], got_x.at[k, 0], rx_s.at[k, 0], rx_r.at[k, 0], toward(ways(k)))
    for k in range(NZ):
        for dx in (0, 1, -1):
            pick(tile_at(k, dx))

    def pass_on(k):
        arrive(got_x.at[k, 0], rx_r.at[k, 0])
        mid_x[k] = (got_x[k, 0].astype(F32) + part[tile_at(k, ways(k))].astype(F32)).astype(BF)
        start(mid_x.at[k], got_x.at[k, 1], rx_s.at[k, 1], rx_r.at[k, 1], toward(ways(k)))
        start(part.at[tile_at(k, -ways(k))], got_x.at[k, 2], rx_s.at[k, 2], rx_r.at[k, 2],
              toward(-ways(k)))

    def sum_x(k):
        arrive(got_x.at[k, 1], rx_r.at[k, 1])
        arrive(got_x.at[k, 2], rx_r.at[k, 2])
        value = part[tile_at(k)].astype(F32) + got_x[k, 1].astype(F32) + got_x[k, 2].astype(F32)
        if k < NZ - 1:
            sum_z[k] = value.astype(BF)
            slot = lax.rem(me.z - at_z[k] + NZ, NZ)
            start(sum_z.at[k], got_z.at[slot], rz_s.at[k], rz_r.at[slot], (me.b, at_z[k] * NX + me.x))
        return value

    for i in range(NZ + 2):
        if i < NZ:
            pass_on(i)
        if i >= 2:
            value = sum_x(i - 2)
    turn(0, BLOCKS // 2)
    for o in range(1, NZ):
        arrive(got_z.at[o], rz_r.at[o])
        value += got_z[o].astype(F32)

    load_cot.wait()
    agg = value.astype(BF)
    pre = jnp.dot(agg, weight[...], preferred_element_type=F32)
    sig = jax.nn.sigmoid(pre)
    dpre = (cot[...].astype(F32) * sig * (1.0 + pre * (1.0 - sig))).astype(BF)
    back[me.r] = lax.dot_general(
        dpre, weight[...], (((1,), (1,)), ((), ())), preferred_element_type=F32
    ).astype(BF)

    at_z.reverse()

    def over_x(k):
        slot = back.at[tile_at(k)]
        for dx in (1, -1):
            start(slot, slot, gx_s.at[k, dx % NX], gx_r.at[k, dx % NX], toward(dx))

    def relay(k):
        way = ways(k)
        slot = back.at[tile_at(k, -way)]
        arrive(slot, gx_r.at[k, way % NX])
        start(slot, slot, gx_s.at[k, 2], gx_r.at[k, 2], toward(way))

    mine_back = back.at[me.r]
    over_x(0)
    for k in range(1, NZ):
        start(mine_back, mine_back, gz_s.at[k], gz_r.at[me.z], (me.b, at_z[k] * NX + me.x))

    act_out[...] = (pre * sig).astype(BF)
    wsum[...] = lax.dot_general(agg, dpre, (((0,), (0,)), ((), ())), preferred_element_type=F32)
    half = SIDE
    w1_out[...] = wsum[pl.ds((1 - me.c) * half, half), :].astype(BF)
    start(w1_out, w1_in, wa_s.at[0], wa_r.at[0], sibling)

    def from_z(k):
        arrive(back.at[tile_at(k)], gz_r.at[at_z[k]])
        over_x(k)

    from_z(1)
    relay(0)
    from_z(2)
    arrive(w1_in, wa_r.at[0])
    w1 = wsum[pl.ds(me.c * half, half), :] + w1_in[...].astype(F32)
    wsum[0:half, :] = w1
    w2_out[...] = w1.astype(BF).reshape(NY, 16, WIDTH)
    for dy in range(1, NY):
        start(w2_out.at[lax.rem(me.y + dy, NY)], w2_in.at[dy], wy_s.at[dy], wy_r.at[dy],
              (me.blk(dy=dy), me.r))
    turn(BLOCKS // 2, 3 * BLOCKS // 4)
    for k in range(3, NZ):
        from_z(k)
        relay(k - 2)
    relay(NZ - 2)
    turn(3 * BLOCKS // 4, BLOCKS)
    relay(NZ - 1)

    w2 = wsum[pl.ds(me.y * 16, 16), :]
    for dy in range(1, NY):
        arrive(w2_in.at[dy], wy_r.at[dy])
        w2 += w2_in[dy].astype(F32)
    w3_in[me.x] = w2.astype(BF)
    for dx in range(1, NX):
        slot = w3_in.at[me.x]
        start(slot, slot, wx_s.at[dx], wx_r.at[dx], (me.b, me.rep(dx=dx)))

    for k in range(NZ):
        arrive(back.at[tile_at(k, ways(k))], gx_r.at[k, -ways(k) % NX])
        arrive(back.at[tile_at(k, 2)], gx_r.at[k, 2])

    def term(c):
        picked = jnp.concatenate([back[target(c, k)] for k in range(SLOTS)], axis=0)
        return jnp.dot(tiles_t[c], picked, preferred_element_type=F32)

    def to_sibling(p):
        return remote(to_core.at[p], from_core.at[p], core_s.at[p], core_r.at[p], sibling)

    def terms(p, carry):
        e, dy = (choose(p, v) for v in zip(*GROUPS))
        y = lax.rem(me.y + dy + NY, NY)
        h = jnp.where(e == 1, 1 - me.h, me.h)
        base = (y * 2 + h) * 2
        to_core[p] = term(base + 1 - me.c).astype(BF)
        to_sibling(p).start()
        mine[p] = term(base + me.c)
        return carry

    def both(e, dy):
        p = GROUPS.index((e, dy))
        to_sibling(p).wait_recv()
        return mine[p] + from_core[p].astype(F32)

    def hop(e, dy, value):
        k = HOPS.index((e, dy))
        ring_out[k] = value.astype(BF)
        step = dy if abs(dy) < 3 else (dy - 2 if dy > 0 else dy + 2)
        if dy == 4 and e == 0:
            step = -2
        start(ring_out.at[k], ring_in.at[k], ring_s.at[k], ring_r.at[k], (me.blk(dy=step), me.r))

    def landed(e, dy):
        k = HOPS.index((e, dy))
        arrive(ring_in.at[k], ring_r.at[k])
        return ring_in[k].astype(F32)

    def far_hops(e):
        for sign in (1, -1):
            value = both(e, 2 * sign) + landed(e, 3 * sign)
            if (sign > 0) == (e == 1):
                value += landed(e, 4)
            hop(e, 2 * sign, value)

    def owned(e):
        value = both(e, 0)
        for dy in (1, -1, 2, -2):
            value += landed(e, dy)
        return value

    lax.fori_loop(0, 6, terms, 0)
    for e, dy in GROUPS[:6]:
        hop(e, dy, both(e, dy))
    lax.fori_loop(6, 16, terms, 0)

    w3 = None
    for dx in range(1, NX):
        slot = w3_in.at[lax.rem(me.x + NX - dx, NX)]
        arrive(slot, wx_r.at[dx])
    w3 = sum((w3_in[i].astype(F32) for i in range(1, NX)), w3_in[0].astype(F32))
    zed = me.h * NZ + me.z
    w4_in[zed] = w3.astype(BF)
    for e in (0, 1):
        for dz in range(NZ):
            if e or dz:
                slot = w4_in.at[zed]
                start(slot, slot, wz_s.at[e, dz], wz_r.at[e, dz], (me.blk(e=e), me.rep(dz=dz)))

    far_hops(1)
    for dy in (1, -1):
        hop(1, dy, both(1, dy))
    far_hops(0)
    for dy in (1, -1):
        hop(0, dy, both(0, dy))

    for e in (0, 1):
        for dz in range(NZ):
            if e or dz:
                h = 1 - me.h if e else me.h
                slot = w4_in.at[h * NZ + lax.rem(me.z + NZ - dz, NZ)]
                arrive(slot, wz_r.at[e, dz])
    w4 = sum((w4_in[i].astype(F32) for i in range(1, 2 * NZ)), w4_in[0].astype(F32))
    w5_in[me.y] = w4.astype(BF)

    cross_out[...] = owned(1).astype(BF)
    start(cross_out, cross_in, cross_s.at[0], cross_r.at[0], other)
    for dy in range(1, NY):
        slot = w5_in.at[me.y]
        start(slot, slot, wo_s.at[dy], wo_r.at[dy], (me.blk(dy=dy), me.r))
    value = owned(0)
    for dy in range(1, NY):
        arrive(w5_in.at[lax.rem(me.y + NY - dy, NY)], wo_r.at[dy])
    start(w5_in, w6_in, wa_s.at[1], wa_r.at[1], sibling)
    weight_out[pl.ds(me.c * half, half), :] = w5_in[...].astype(F32).reshape(half, WIDTH)
    arrive(w6_in, wa_r.at[1])
    weight_out[pl.ds((1 - me.c) * half, half), :] = w6_in[...].astype(F32).reshape(half, WIDTH)
    arrive(cross_in, cross_r.at[0])
    grad_out[...] = (value + cross_in[...].astype(F32)).astype(BF)
    for copy in sends:
        copy.wait_send()

    def drain(p, carry):
        to_sibling(p).wait_send()
        return carry

    lax.fori_loop(0, 16, drain, 0)


def dma(*shape):
    return pltpu.SemaphoreType.DMA(shape)


def piece(*lead, dtype=BF):
    return pltpu.VMEM((*lead, SIDE, WIDTH), dtype)


def body(features, tiles, tile_rows, tile_count, weight, cotangent):
    small = pltpu.VMEM((NY, 16, WIDTH), BF)
    return pl.pallas_call(
        layer_kernel,
        out_shape=(
            jax.ShapeDtypeStruct((SIDE, WIDTH), BF),
            jax.ShapeDtypeStruct((SIDE, WIDTH), BF),
            jax.ShapeDtypeStruct((WIDTH, WIDTH), F32),
        ),
        in_specs=[SMEM, SMEM, ANY, ANY, VMEM, ANY],
        out_specs=(VMEM, VMEM, VMEM),
        scratch_shapes=[
            piece(BLOCKS),
            pltpu.VMEM((BLOCKS, SLOTS, SIDE, SIDE), BF),
            pltpu.VMEM((BLOCKS, SIDE, SLOTS * SIDE), BF),
            piece(BLOCKS * SLOTS, dtype=F32),
            piece(BLOCKS * SLOTS + 1),
            piece(PARTS),
            pltpu.VMEM((4, 8, SIDE), jnp.int32),
            pltpu.SMEM((4, 8, SIDE), jnp.int32),
            piece(),
            piece(NZ, 3), piece(NZ), piece(NZ), piece(NZ),
            piece(PARTS + 1),
            piece(16), piece(16), piece(16, dtype=F32),
            piece(len(HOPS)), piece(len(HOPS)),
            piece(), piece(),
            pltpu.VMEM((WIDTH, WIDTH), F32),
            piece(), piece(),
            small, small,
            pltpu.VMEM((NX, 16, WIDTH), BF),
            pltpu.VMEM((2 * NZ, 16, WIDTH), BF),
            small, small,
            dma(4), dma(6, BLOCKS), dma(BLOCKS),
            dma(NZ, 3), dma(NZ, 3), dma(NZ), dma(NZ),
            dma(NZ), dma(NZ), dma(NZ, NX), dma(NZ, NX),
            dma(16), dma(16), dma(len(HOPS)), dma(len(HOPS)),
            dma(1), dma(1), dma(2), dma(2),
            dma(NY), dma(NY), dma(NX), dma(NX), dma(2, NZ), dma(2, NZ), dma(NY), dma(NY),
        ],
        compiler_params=pltpu.CompilerParams(
            collective_id=0, has_side_effects=True, vmem_limit_bytes=58 << 20
        ),
        name="graph_layer",
    )(tile_rows[0, :, 0].T, tile_count[0, :, 0], features, tiles, weight, cotangent)


def solution(mesh):
    placed = (
        P("blk", None),
        P("blk", None, "rep", None, None, None),
        P("blk", None, "rep", None),
        P("blk", None, "rep"),
        P(),
        P("blk", None),
    )
    return jax.shard_map(
        body,
        mesh=mesh,
        in_specs=placed,
        out_specs=(P(("blk", "rep"), None), P(("blk", "rep"), None), P()),
        check_vma=False,
    )
```

time: 143 us -> 126 us (0.88)
  the two profiles are of different devices: /device:TPU:4 before, /device:TPU:15 now
where the time goes in v2:
time: 126 us; the launch traced here: 125 us
  Pallas kernels  120 us (95%)
  local copies, waits for them, and re-layouts  4.61 us (4%)
    pallas_call x1, Pallas kernels, body(): pl.pallas_call(layer_kernel, out_shape=(jax.ShapeDtypeStruct((SIDE, WIDTH...  120 us
    unnamed x3, local copies, waits for them, and re-layouts  4.61 us

profile of v2, /device:TPU:15, one launch (start us, length us, event | category | flops | bytes accessed | tf_op | source)
XLA Modules:
  0.0 125.2 jit_solution(8177960994549994215)
XLA Ops:
  0.6 120.0 %graph_layer.1 = (bf16[128,256]{1,0:T(8,128)(2,1)}, bf16[128,256]{1,0:T(8,128)(2,1)}, f32[256,256]{1,0:T(8,128)}) custom-call(s32[4,32]{1,0:T(4,128)} %bitcast.4, s32[32]{0:T(128)} %bitcast.5, bf16[3072,256]{1,0:T(8,128)(2,1)} %feat.1, bf16[1,32,1,4,128,128]{5,4,3,2,1,0:T(8,128)(2,1)} %tiles_hbm.1, bf16[256,256]{1,0:T(8,128)(2,1)} %weight.1, ...), custom_call_target="tpu_custom_call" | custom-call | tf_op jit(solution)/shard_map/graph_layer/pallas_call | solution.py:452
  120.6 1.5 %copy.12 = bf16[128,256]{1,0:T(8,128)(2,1)} copy(bf16[128,256]{1,0:T(8,128)(2,1)} %get-tuple-element.6) | data formatting | bytes 131072
  122.1 1.5 %copy.13 = bf16[128,256]{1,0:T(8,128)(2,1)} copy(bf16[128,256]{1,0:T(8,128)(2,1)} %get-tuple-element.7) | data formatting | bytes 131072
  123.6 1.7 %copy.14 = f32[256,256]{1,0:T(8,128)} copy(f32[256,256]{1,0:T(8,128)} %get-tuple-element.8) | data formatting | bytes 524288

commit v3 on v2

--- a/solution.py
+++ b/solution.py
@@ -48,7 +48,6 @@
     )
 
 
-NEAR = [sorted((z for z in range(NZ) if z != home), key=lambda z: abs(z - home)) for home in range(NZ)]
 HOPS = [(e, dy) for dy in (4, 3, -3, 2, -2, 1, -1) for e in (1, 0)]
 GROUPS = [(1, 4), (0, 4)] + [(e, s * m) for m in (3, 2, 1) for s in (1, -1) for e in (1, 0)] + [(1, 0), (0, 0)]
 
@@ -160,7 +159,7 @@
             column(c)
             return carry
 
-        lax.fori_loop(0, len(which), body, 0)
+        lax.fori_loop(0, len(which), body, 0, unroll=2)
 
     def onward(e):
         for dy in (-2, 2):
@@ -199,8 +198,8 @@
     early = [(0, 0), (1, 0)] + [(0, dy) for dy in (1, -1, 2, -2)] + [(1, dy) for dy in (1, -1, 2, -2)]
     late = [(0, 3), (0, -3), (0, 4), (1, 3), (1, -3), (1, 4)]
     columns(early + late[:3], 0)
+    columns(early, 1)
     settle(1, 3, -3, 4)
-    columns(early, 1)
     columns(late[3:], 0)
     columns(late, 1)
 
@@ -220,7 +219,15 @@
     def pick(t):
         part[t] = sums[marks_s[3, 0, t]]
 
-    at_z = [choose(me.z, [NEAR[home][NZ - 2 - k] for home in range(NZ)]) for k in range(NZ - 1)] + [me.z]
+    run, spot = lax.div(me.z, 3), lax.rem(me.z, 3)
+
+    def place_z(j, across):
+        return (1 - run if across else run) * 3 + lax.rem(spot + j, 3)
+
+    at_z = [place_z(1, 1), place_z(2, 1), place_z(0, 1), place_z(1, 0), place_z(2, 0), me.z]
+
+    def along(z):
+        return (me.b, z * NX + me.x)
 
     def tile_at(k, dx=0):
         return at_z[k] * NX + lax.rem(me.x + dx + NX, NX)
@@ -249,21 +256,30 @@
         arrive(got_x.at[k, 1], rx_r.at[k, 1])
         arrive(got_x.at[k, 2], rx_r.at[k, 2])
         value = part[tile_at(k)].astype(F32) + got_x[k, 1].astype(F32) + got_x[k, 2].astype(F32)
-        if k < NZ - 1:
-            sum_z[k] = value.astype(BF)
-            slot = lax.rem(me.z - at_z[k] + NZ, NZ)
-            start(sum_z.at[k], got_z.at[slot], rz_s.at[k], rz_r.at[slot], (me.b, at_z[k] * NX + me.x))
+        if k in (0, 1, 3, 4):
+            z_send(k, value, place_z(k % 3 + 1, 0))
         return value
 
+    def z_send(k, value, z):
+        sum_z[k] = value.astype(BF)
+        start(sum_z.at[k], got_z.at[k], rz_s.at[k], rz_r.at[k], along(z))
+
+    def z_got(k):
+        arrive(got_z.at[k], rz_r.at[k])
+        return got_z[k].astype(F32)
+
+    totals = {}
     for i in range(NZ + 2):
         if i < NZ:
             pass_on(i)
         if i >= 2:
-            value = sum_x(i - 2)
+            totals[i - 2] = sum_x(i - 2)
+        if i == 5:
+            z_send(2, totals[2] + z_got(0) + z_got(1), place_z(0, 1))
     turn(0, BLOCKS // 2)
-    for o in range(1, NZ):
-        arrive(got_z.at[o], rz_r.at[o])
-        value += got_z[o].astype(F32)
+    value = totals[NZ - 1]
+    for k in (3, 4, 2):
+        value += z_got(k)
 
     load_cot.wait()
     agg = value.astype(BF)
@@ -274,7 +290,7 @@
         dpre, weight[...], (((1,), (1,)), ((), ())), preferred_element_type=F32
     ).astype(BF)
 
-    at_z.reverse()
+    at_z = [me.z, place_z(1, 0), place_z(2, 0), place_z(0, 1), place_z(1, 1), place_z(2, 1)]
 
     def over_x(k):
         slot = back.at[tile_at(k)]
@@ -288,9 +304,9 @@
         start(slot, slot, gx_s.at[k, 2], gx_r.at[k, 2], toward(way))
 
     mine_back = back.at[me.r]
+    for k in (3, 2, 1):
+        start(mine_back, mine_back, gz_s.at[k], gz_r.at[me.z], along(at_z[k]))
     over_x(0)
-    for k in range(1, NZ):
-        start(mine_back, mine_back, gz_s.at[k], gz_r.at[me.z], (me.b, at_z[k] * NX + me.x))
 
     act_out[...] = (pre * sig).astype(BF)
     wsum[...] = lax.dot_general(agg, dpre, (((0,), (0,)), ((), ())), preferred_element_type=F32)
@@ -299,12 +315,16 @@
     start(w1_out, w1_in, wa_s.at[0], wa_r.at[0], sibling)
 
     def from_z(k):
-        arrive(back.at[tile_at(k)], gz_r.at[at_z[k]])
+        slot = back.at[tile_at(k)]
+        arrive(slot, gz_r.at[at_z[k]])
+        if k == 3:
+            for j in (2, 1):
+                start(slot, slot, gz_s.at[3 + j], gz_r.at[at_z[k]], along(at_z[j]))
         over_x(k)
 
-    from_z(1)
+    for k in (3, 1, 2):
+        from_z(k)
     relay(0)
-    from_z(2)
     arrive(w1_in, wa_r.at[0])
     w1 = wsum[pl.ds(me.c * half, half), :] + w1_in[...].astype(F32)
     wsum[0:half, :] = w1
@@ -313,12 +333,13 @@
         start(w2_out.at[lax.rem(me.y + dy, NY)], w2_in.at[dy], wy_s.at[dy], wy_r.at[dy],
               (me.blk(dy=dy), me.r))
     turn(BLOCKS // 2, 3 * BLOCKS // 4)
-    for k in range(3, NZ):
+    for k in (4, 5):
         from_z(k)
-        relay(k - 2)
-    relay(NZ - 2)
+    for k in (1, 2, 3):
+        relay(k)
     turn(3 * BLOCKS // 4, BLOCKS)
-    relay(NZ - 1)
+    for k in (4, 5):
+        relay(k)
 
     w2 = wsum[pl.ds(me.y * 16, 16), :]
     for dy in range(1, NY):
@@ -381,10 +402,10 @@
             value += landed(e, dy)
         return value
 
-    lax.fori_loop(0, 6, terms, 0)
+    lax.fori_loop(0, 6, terms, 0, unroll=2)
     for e, dy in GROUPS[:6]:
         hop(e, dy, both(e, dy))
-    lax.fori_loop(6, 16, terms, 0)
+    lax.fori_loop(6, 16, terms, 0, unroll=2)
 
     w3 = None
     for dx in range(1, NX):

time: 126 us -> 119 us (0.944)
  the two profiles are of different devices: /device:TPU:15 before, /device:TPU:2 now
where the time goes in v3:
time: 119 us
  Pallas kernels  114 us (96%)
  local copies, waits for them, and re-layouts  4.61 us (4%)
    pallas_call x1, Pallas kernels, body(): pl.pallas_call(layer_kernel, out_shape=(jax.ShapeDtypeStruct((SIDE, WIDTH...  114 us
    unnamed x3, local copies, waits for them, and re-layouts  4.61 us

profile of v3, /device:TPU:2, one launch (start us, length us, event | category | flops | bytes accessed | tf_op | source)
XLA Modules:
  0.0 119.0 jit_solution(12248836202516230983)
XLA Ops:
  0.6 113.8 %graph_layer.1 = (bf16[128,256]{1,0:T(8,128)(2,1)}, bf16[128,256]{1,0:T(8,128)(2,1)}, f32[256,256]{1,0:T(8,128)}) custom-call(s32[4,32]{1,0:T(4,128)} %bitcast.4, s32[32]{0:T(128)} %bitcast.5, bf16[3072,256]{1,0:T(8,128)(2,1)} %feat.1, bf16[1,32,1,4,128,128]{5,4,3,2,1,0:T(8,128)(2,1)} %tiles_hbm.1, bf16[256,256]{1,0:T(8,128)(2,1)} %weight.1, ...), custom_call_target="tpu_custom_call" | custom-call | tf_op jit(solution)/shard_map/graph_layer/pallas_call | solution.py:473
  114.4 1.5 %copy.12 = bf16[128,256]{1,0:T(8,128)(2,1)} copy(bf16[128,256]{1,0:T(8,128)(2,1)} %get-tuple-element.6) | data formatting | bytes 131072
  115.9 1.5 %copy.13 = bf16[128,256]{1,0:T(8,128)(2,1)} copy(bf16[128,256]{1,0:T(8,128)(2,1)} %get-tuple-element.7) | data formatting | bytes 131072
  117.4 1.7 %copy.14 = f32[256,256]{1,0:T(8,128)} copy(f32[256,256]{1,0:T(8,128)} %get-tuple-element.8) | data formatting | bytes 524288

commit v4 on v3

--- a/solution.py
+++ b/solution.py
@@ -186,6 +186,12 @@
     marks[0] = lax.fori_loop(0, SIDE, rank_of, nought, unroll=8)
     marks[3] = jnp.where(upto > below, upto - 1, SIDE)
     pltpu.sync_copy(marks.at[0], marks_s.at[0])
+    load_tiles.wait()
+    load_own.wait()
+    first = [(0, 0), (1, 0)] + [(0, dy) for dy in (1, -1, 2, -2)]
+    second = [(1, dy) for dy in (1, -1, 2, -2)] + [(0, dy) for dy in (3, -3, 4)]
+    last = [(1, dy) for dy in (3, -3, 4)]
+    columns(first, 0)
     onward(1)
     settle(1, 1, -1)
     settle(0, 3, -3, 4)
@@ -193,15 +199,12 @@
     marks[1] = order
     marks[2] = keys
     pltpu.sync_copy(marks.at[pl.ds(1, 3)], marks_s.at[pl.ds(1, 3)])
-    load_tiles.wait()
-    load_own.wait()
-    early = [(0, 0), (1, 0)] + [(0, dy) for dy in (1, -1, 2, -2)] + [(1, dy) for dy in (1, -1, 2, -2)]
-    late = [(0, 3), (0, -3), (0, 4), (1, 3), (1, -3), (1, 4)]
-    columns(early + late[:3], 0)
-    columns(early, 1)
+    columns(first, 1)
+    columns(second, 0)
     settle(1, 3, -3, 4)
-    columns(late[3:], 0)
-    columns(late, 1)
+    columns(second, 1)
+    columns(last, 0)
+    columns(last, 1)
 
     for lo in range(0, SIDE, 64):
         span = slice(lo, lo + 64)
@@ -269,12 +272,11 @@
         return got_z[k].astype(F32)
 
     totals = {}
-    for i in range(NZ + 2):
-        if i < NZ:
-            pass_on(i)
-        if i >= 2:
-            totals[i - 2] = sum_x(i - 2)
-        if i == 5:
+    for k in range(NZ):
+        pass_on(k)
+    for k in range(NZ):
+        totals[k] = sum_x(k)
+        if k == 3:
             z_send(2, totals[2] + z_got(0) + z_got(1), place_z(0, 1))
     turn(0, BLOCKS // 2)
     value = totals[NZ - 1]
@@ -337,10 +339,6 @@
         from_z(k)
     for k in (1, 2, 3):
         relay(k)
-    turn(3 * BLOCKS // 4, BLOCKS)
-    for k in (4, 5):
-        relay(k)
-
     w2 = wsum[pl.ds(me.y * 16, 16), :]
     for dy in range(1, NY):
         arrive(w2_in.at[dy], wy_r.at[dy])
@@ -350,64 +348,10 @@
         slot = w3_in.at[me.x]
         start(slot, slot, wx_s.at[dx], wx_r.at[dx], (me.b, me.rep(dx=dx)))
 
-    for k in range(NZ):
-        arrive(back.at[tile_at(k, ways(k))], gx_r.at[k, -ways(k) % NX])
-        arrive(back.at[tile_at(k, 2)], gx_r.at[k, 2])
-
-    def term(c):
-        picked = jnp.concatenate([back[target(c, k)] for k in range(SLOTS)], axis=0)
-        return jnp.dot(tiles_t[c], picked, preferred_element_type=F32)
-
-    def to_sibling(p):
-        return remote(to_core.at[p], from_core.at[p], core_s.at[p], core_r.at[p], sibling)
-
-    def terms(p, carry):
-        e, dy = (choose(p, v) for v in zip(*GROUPS))
-        y = lax.rem(me.y + dy + NY, NY)
-        h = jnp.where(e == 1, 1 - me.h, me.h)
-        base = (y * 2 + h) * 2
-        to_core[p] = term(base + 1 - me.c).astype(BF)
-        to_sibling(p).start()
-        mine[p] = term(base + me.c)
-        return carry
-
-    def both(e, dy):
-        p = GROUPS.index((e, dy))
-        to_sibling(p).wait_recv()
-        return mine[p] + from_core[p].astype(F32)
-
-    def hop(e, dy, value):
-        k = HOPS.index((e, dy))
-        ring_out[k] = value.astype(BF)
-        step = dy if abs(dy) < 3 else (dy - 2 if dy > 0 else dy + 2)
-        if dy == 4 and e == 0:
-            step = -2
-        start(ring_out.at[k], ring_in.at[k], ring_s.at[k], ring_r.at[k], (me.blk(dy=step), me.r))
-
-    def landed(e, dy):
-        k = HOPS.index((e, dy))
-        arrive(ring_in.at[k], ring_r.at[k])
-        return ring_in[k].astype(F32)
-
-    def far_hops(e):
-        for sign in (1, -1):
-            value = both(e, 2 * sign) + landed(e, 3 * sign)
-            if (sign > 0) == (e == 1):
-                value += landed(e, 4)
-            hop(e, 2 * sign, value)
-
-    def owned(e):
-        value = both(e, 0)
-        for dy in (1, -1, 2, -2):
-            value += landed(e, dy)
-        return value
-
-    lax.fori_loop(0, 6, terms, 0, unroll=2)
-    for e, dy in GROUPS[:6]:
-        hop(e, dy, both(e, dy))
-    lax.fori_loop(6, 16, terms, 0, unroll=2)
-
-    w3 = None
+    turn(3 * BLOCKS // 4, BLOCKS)
+    for k in (4, 5):
+        relay(k)
+
     for dx in range(1, NX):
         slot = w3_in.at[lax.rem(me.x + NX - dx, NX)]
         arrive(slot, wx_r.at[dx])
@@ -420,13 +364,69 @@
                 slot = w4_in.at[zed]
                 start(slot, slot, wz_s.at[e, dz], wz_r.at[e, dz], (me.blk(e=e), me.rep(dz=dz)))
 
+    for k in range(NZ):
+        arrive(back.at[tile_at(k, ways(k))], gx_r.at[k, -ways(k) % NX])
+        arrive(back.at[tile_at(k, 2)], gx_r.at[k, 2])
+
+    def term(c):
+        picked = jnp.concatenate([back[target(c, k)] for k in range(SLOTS)], axis=0)
+        return jnp.dot(tiles_t[c], picked, preferred_element_type=F32)
+
+    def to_sibling(p):
+        return remote(to_core.at[p], from_core.at[p], core_s.at[p], core_r.at[p], sibling)
+
+    def terms(p, carry):
+        e, dy = (choose(p, v) for v in zip(*GROUPS))
+        y = lax.rem(me.y + dy + NY, NY)
+        h = jnp.where(e == 1, 1 - me.h, me.h)
+        base = (y * 2 + h) * 2
+        to_core[p] = term(base + 1 - me.c).astype(BF)
+        to_sibling(p).start()
+        mine[p] = term(base + me.c)
+        return carry
+
+    def both(e, dy):
+        p = GROUPS.index((e, dy))
+        to_sibling(p).wait_recv()
+        return mine[p] + from_core[p].astype(F32)
+
+    def hop(e, dy, value):
+        k = HOPS.index((e, dy))
+        ring_out[k] = value.astype(BF)
+        step = dy if abs(dy) < 3 else (dy - 2 if dy > 0 else dy + 2)
+        if dy == 4 and e == 0:
+            step = -2
+        start(ring_out.at[k], ring_in.at[k], ring_s.at[k], ring_r.at[k], (me.blk(dy=step), me.r))
+
+    def landed(e, dy):
+        k = HOPS.index((e, dy))
+        arrive(ring_in.at[k], ring_r.at[k])
+        return ring_in[k].astype(F32)
+
+    def far_hops(e):
+        for sign in (1, -1):
+            value = both(e, 2 * sign) + landed(e, 3 * sign)
+            if (sign > 0) == (e == 1):
+                value += landed(e, 4)
+            hop(e, 2 * sign, value)
+
+    def owned(e):
+        value = both(e, 0)
+        for dy in (1, -1, 2, -2):
+            value += landed(e, dy)
+        return value
+
+    lax.fori_loop(0, 6, terms, 0, unroll=2)
+    for e, dy in GROUPS[:6]:
+        hop(e, dy, both(e, dy))
+    lax.fori_loop(6, 16, terms, 0, unroll=2)
+
     far_hops(1)
     for dy in (1, -1):
         hop(1, dy, both(1, dy))
     far_hops(0)
     for dy in (1, -1):
         hop(0, dy, both(0, dy))
-
     for e in (0, 1):
         for dz in range(NZ):
             if e or dz:
@@ -435,12 +435,12 @@
                 arrive(slot, wz_r.at[e, dz])
     w4 = sum((w4_in[i].astype(F32) for i in range(1, 2 * NZ)), w4_in[0].astype(F32))
     w5_in[me.y] = w4.astype(BF)
-
-    cross_out[...] = owned(1).astype(BF)
-    start(cross_out, cross_in, cross_s.at[0], cross_r.at[0], other)
     for dy in range(1, NY):
         slot = w5_in.at[me.y]
         start(slot, slot, wo_s.at[dy], wo_r.at[dy], (me.blk(dy=dy), me.r))
+
+    cross_out[...] = owned(1).astype(BF)
+    start(cross_out, cross_in, cross_s.at[0], cross_r.at[0], other)
     value = owned(0)
     for dy in range(1, NY):
         arrive(w5_in.at[lax.rem(me.y + NY - dy, NY)], wo_r.at[dy])

time: 119 us -> 119 us (level)
  the two profiles are of different devices: /device:TPU:2 before, /device:TPU:8 now
where the time goes in v4:
time: 119 us
  Pallas kernels  113 us (95%)
  local copies, waits for them, and re-layouts  4.61 us (4%)
    pallas_call x1, Pallas kernels, body(): pl.pallas_call(layer_kernel, out_shape=(jax.ShapeDtypeStruct((SIDE, WIDTH...  113 us
    unnamed x3, local copies, waits for them, and re-layouts  4.61 us

profile of v4, /device:TPU:8, one launch (start us, length us, event | category | flops | bytes accessed | tf_op | source)
XLA Modules:
  0.0 118.7 jit_solution(17981641752779233163)
XLA Ops:
  0.6 113.5 %graph_layer.1 = (bf16[128,256]{1,0:T(8,128)(2,1)}, bf16[128,256]{1,0:T(8,128)(2,1)}, f32[256,256]{1,0:T(8,128)}) custom-call(s32[4,32]{1,0:T(4,128)} %bitcast.4, s32[32]{0:T(128)} %bitcast.5, bf16[3072,256]{1,0:T(8,128)(2,1)} %feat.1, bf16[1,32,1,4,128,128]{5,4,3,2,1,0:T(8,128)(2,1)} %tiles_hbm.1, bf16[256,256]{1,0:T(8,128)(2,1)} %weight.1, ...), custom_call_target="tpu_custom_call" | custom-call | tf_op jit(solution)/shard_map/graph_layer/pallas_call | solution.py:473
  114.1 1.5 %copy.12 = bf16[128,256]{1,0:T(8,128)(2,1)} copy(bf16[128,256]{1,0:T(8,128)(2,1)} %get-tuple-element.6) | data formatting | bytes 131072
  115.6 1.5 %copy.13 = bf16[128,256]{1,0:T(8,128)(2,1)} copy(bf16[128,256]{1,0:T(8,128)(2,1)} %get-tuple-element.7) | data formatting | bytes 131072
  117.1 1.7 %copy.14 = f32[256,256]{1,0:T(8,128)} copy(f32[256,256]{1,0:T(8,128)} %get-tuple-element.8) | data formatting | bytes 524288
